TPU v7x, 256 devices: a whole 4x4x8 slice. The times are simulated.
256 devices in a mesh: dp: 2 (over x_lo), seq: 16 (over z, core), fsdp: 8 (over x_hi, y).
Axes of the slice: x: 4 (x_hi: 2, x_lo: 2; x = x_hi * 2 + x_lo), y: 4, z: 8, core: 2. Of those that a mesh axis runs over, the one named last changes fastest.
Arguments:
- queries_raw: bfloat16 [16, 4096, 2048], P(('dp', 'fsdp'), 'seq'), parts along dimension 0, may hold values from -6 to 6
- keys_values: bfloat16 [16, 4096, 2048], P(('dp', 'fsdp'), 'seq'), parts along dimension 0, may hold values from -6 to 6
- doc_ids: int32 [16, 4096], P(('dp', 'fsdp')), parts along dimension 0, may hold values from 0 to 3, never falling along the last dimension, each value on 1 to 2048 neighbouring positions
- q_gain: float32 [128], replicated, may hold values from 0.6 to 7
- k_gain: float32 [128], replicated, may hold values from 0.6 to 7
- out_weight: bfloat16 [2048, 5376], P('fsdp'), may hold values from -0.125 to 0.125
- post_gain: float32 [5376], replicated, may hold values from 0.25 to 1.75
Outputs:
- layer_out: bfloat16 [16, 4096, 5376], P(('dp', 'fsdp'), 'seq'), parts along dimension 0
There are 2 independent parts, one for each index of `dp`. A program takes and returns all parts, laid end to end along the dimension named above; an argument that names none is the same for every part. Nothing has to cross between parts.
Inputs may be any that keep to these rules, and one draw needn't show every extreme that they name: `doc_ids`: each slab's document numbers never fall; a document has at most 2048 tokens, and one has exactly that many.
All inputs are finite; a program needn't handle non-finite values.
Results may differ from a plain program's by a relative error of at most 0.008.
The roundings to bfloat16 on the way count: a program that leaves them out, or rounds other values in their place, can miss the bound.
Values may be sent and summed in bfloat16 or wider, within the bound.
No kernel may reach another device: no remote copies, remote signals or barrier semaphores. Data moves between devices by JAX's collectives and lax.ppermute only.
A program may use at most 128 MiB of HBM per device.

v0:
```python
import math
import jax
import jax.numpy as jnp
from jax import lax
from jax.sharding import PartitionSpec as P

WINDOW = 1024
attn_scale = 168.0 ** (-0.5)
norm_eps = 1e-06


def from_behind(block, axis, distance):
    devices = range(lax.axis_size(axis))
    route = [(i - distance, i) for i in devices if i - distance in devices]
    return lax.ppermute(block, axis, route)


def doc_positions(ids):
    count = ids.shape[0]
    index = jnp.arange(count, dtype=jnp.int32)
    flags = jnp.concatenate([jnp.ones((1,), bool), ids[1:] != ids[:-1]])
    starts = lax.cummax(jnp.where(flags, index, 0), axis=0)
    return index - starts


def norm_rope(inputs, gain, positions):
    values = inputs.astype(jnp.float32)
    meansq = jnp.mean(values * values, axis=-1, keepdims=True)
    scaled = values * lax.rsqrt(meansq + norm_eps) * gain
    width = values.shape[-1]
    half = width // 2
    inverse = 10000.0 ** (-(jnp.arange(half, dtype=jnp.float32) * 2.0 / width))
    angles = positions.astype(jnp.float32)[:, None] * inverse[None, :]
    cosine = jnp.cos(angles)[:, None, :]
    sine = jnp.sin(angles)[:, None, :]
    first = scaled[..., :half]
    second = scaled[..., half:]
    rotated = jnp.concatenate(
        [first * cosine - second * sine, second * cosine + first * sine], axis=-1
    )
    return rotated.astype(jnp.bfloat16)


def on_device(queries_raw, keys_values, doc_ids, q_gain, k_gain, out_weight, post_gain):
    tokens = queries_raw.shape[1]
    head_dim = q_gain.shape[0]
    features = queries_raw.shape[2]
    heads = features // head_dim
    kv_cols = keys_values.shape[2] // 2
    kv_heads = kv_cols // head_dim
    group = heads // kv_heads
    seq_index = lax.axis_index("seq")
    begin = seq_index * tokens
    ids_all = doc_ids[0]
    positions = lax.dynamic_slice_in_dim(doc_positions(ids_all), begin, tokens, 0)
    queries = norm_rope(queries_raw[0].reshape(tokens, heads, head_dim), q_gain, positions)
    queries = queries.reshape(tokens, kv_heads, group, head_dim)
    raw_pairs = keys_values[0]
    keys = norm_rope(raw_pairs[:, :kv_cols].reshape(tokens, kv_heads, head_dim), k_gain, positions)
    local = jnp.concatenate([keys.reshape(tokens, kv_cols), raw_pairs[:, kv_cols:]], axis=1)
    reach = (WINDOW - 2) // tokens + 1
    pieces = []
    for offset in range(reach, 0, -1):
        pieces.append(from_behind(local, "seq", offset))
    pieces.append(local)
    joined = jnp.concatenate(pieces, axis=0)
    span = (reach + 1) * tokens
    ids_pad = jnp.concatenate([jnp.full((reach * tokens,), -1, jnp.int32), ids_all])
    key_ids = lax.dynamic_slice_in_dim(ids_pad, begin, span, 0)
    query_ids = lax.dynamic_slice_in_dim(ids_all, begin, tokens, 0)
    key_rows = joined[:, :kv_cols].reshape(span, kv_heads, head_dim)
    value_rows = joined[:, kv_cols:].reshape(span, kv_heads, head_dim)
    block = math.gcd(tokens, 512)
    relative = (
        reach * tokens
        + jnp.arange(block, dtype=jnp.int32)[:, None]
        - jnp.arange(span, dtype=jnp.int32)[None, :]
    )
    allowed = (relative >= 0) & (relative < WINDOW) & (query_ids[0:block, None] == key_ids[None, :])
    scores = (
        jnp.einsum("tkgd,ukd->kgtu", queries, key_rows, preferred_element_type=jnp.float32)
        * attn_scale
    )
    scores = jnp.where(allowed[None, None], scores, -jnp.inf)
    top = jnp.max(scores, axis=-1, keepdims=True)
    expd = jnp.exp(scores - top)
    total = jnp.sum(expd, axis=-1, keepdims=True)
    probs = (expd / total).astype(jnp.bfloat16)
    mixed = jnp.einsum("kgtu,ukd->tkgd", probs, value_rows, preferred_element_type=jnp.float32)
    outputs = mixed.reshape(block, features).astype(jnp.bfloat16)
    n_fsdp = lax.axis_size("fsdp")
    n_seq = lax.axis_size("seq")
    each = out_weight.shape[0] // n_seq
    mine = lax.dynamic_slice_in_dim(out_weight, begin // tokens * each, each, 0)
    arranged = (
        outputs.reshape(tokens, n_fsdp, n_seq, each).transpose(0, 2, 1, 3).reshape(tokens, features)
    )
    partial_rows = lax.all_gather(mine, "fsdp", axis=0, tiled=True)
    all_rows = lax.all_gather(partial_rows, "seq", axis=0, tiled=True)
    projected = jnp.dot(arranged, all_rows, preferred_element_type=jnp.float32)
    meansq = jnp.mean(projected * projected, axis=-1, keepdims=True)
    result = (projected * lax.rsqrt(meansq + norm_eps) * post_gain).astype(jnp.bfloat16)
    return result[None]


def solution(mesh):
    in_specs = (
        P(("dp", "fsdp"), "seq", None),
        P(("dp", "fsdp"), "seq", None),
        P(("dp", "fsdp"), None),
        P(),
        P(),
        P("fsdp", None),
        P(),
    )
    out_specs = P(("dp", "fsdp"), "seq", None)
    return jax.shard_map(
        on_device, mesh=mesh, in_specs=in_specs, out_specs=out_specs, check_vma=False
    )
```

profile of v0, /device:TPU:64, one launch (start us, length us, event | category | flops | bytes accessed | tf_op | source)
XLA Modules:
  0.0 324.0 jit_solution(14192368447268685597)
XLA Ops:
  6.5 1.8 copy-done
  8.3 0.7 constant_dynamic-slice_fusion
  9.1 56.5 %all-gather.3.cloned.1.call-done = bf16[128,5376]{1,0:T(8,128)(2,1)} async-done(((bf16[16,5376]{1,0:T(8,128)(2,1)}), bf16[128,5376]{1,0:T(8,128)(2,1)}) %all-gather.3.cloned.1.call-update) | async-done | bytes 1376272 | tf_op jit(solution)/shard_map/all_gather | solution.py:98
  65.6 0.9 compare_reduce_fusion
  66.5 0.1 add_select_fusion
  66.6 0.3 reduce-window.9
  66.9 0.1 slice.53
  67.0 1.5 copy.26
  68.6 0.1 slice_reduce_fusion
  68.7 0.1 maximum_bitcast_fusion
  68.8 0.1 fusion.11
  68.9 0.1 fusion.9
  69.0 0.3 multiply_cosine_fusion
  69.3 0.2 fusion.10
  69.5 0.1 subtract_convert_fusion.1
  69.7 1.0 pad_maximum_fusion
  70.7 5.7 %collective-permute-start = (bf16[256,2048]{0,1:T(8,128)(2,1)}, bf16[256,2048]{0,1:T(8,128)(2,1)}, u32[]{:S(2)}, u32[]{:S(2)}) collective-permute-start(bf16[256,2048]{0,1:T(8,128)(2,1)} %pad_maximum_fusion), channel_id=1, source_target_pairs={{0,32},{8,40},{16,48},{24,56},{32,64},{40,72},{48,80},{56,88},{64,... | collective-permute-start | bytes 3145736 | tf_op jit(solution)/shard_map/ppermute | solution.py:15
  76.4 1.9 collective-permute-start.1
  78.3 2.6 collective-permute-start.2
  80.9 2.5 collective-permute-start.3
  83.4 0.1 copy.29
  83.5 0.1 copy.30
  83.6 0.2 convert_bitcast_fusion
  83.8 0.4 copy.41
  84.2 0.6 multiply_reduce_fusion.1
  84.9 0.6 add_rsqrt_fusion
  85.5 0.8 copy.28
  86.4 1.4 multiply_multiply_fusion
  87.8 0.8 subtract_convert_fusion
  88.6 1.3 copy.31
  89.9 1.2 copy.32
  91.1 0.1 pad_dynamic-slice_fusion
  91.2 0.5 fusion.8
  91.7 48.3 %collective-permute-done = bf16[256,2048]{0,1:T(8,128)(2,1)} collective-permute-done((bf16[256,2048]{0,1:T(8,128)(2,1)}, bf16[256,2048]{0,1:T(8,128)(2,1)}, u32[]{:S(2)}, u32[]{:S(2)}) %collective-permute-start) | collective-permute-done | bytes 1048608 | tf_op jit(solution)/shard_map/ppermute | solution.py:15
  140.0 1.3 constant_dynamic-update-slice_fusion.4
  141.3 59.7 %collective-permute-done.1 = bf16[256,2048]{0,1:T(8,128)(2,1)} collective-permute-done((bf16[256,2048]{0,1:T(8,128)(2,1)}, bf16[256,2048]{0,1:T(8,128)(2,1)}, u32[]{:S(2)}, u32[]{:S(2)}) %collective-permute-start.1) | collective-permute-done | bytes 1048608 | tf_op jit(solution)/shard_map/ppermute | solution.py:15
  201.0 1.3 constant_dynamic-update-slice_fusion.3
  202.3 43.6 %collective-permute-done.2 = bf16[256,2048]{0,1:T(8,128)(2,1)} collective-permute-done((bf16[256,2048]{0,1:T(8,128)(2,1)}, bf16[256,2048]{0,1:T(8,128)(2,1)}, u32[]{:S(2)}, u32[]{:S(2)}) %collective-permute-start.2) | collective-permute-done | bytes 1048608 | tf_op jit(solution)/shard_map/ppermute | solution.py:15
  245.9 1.3 constant_dynamic-update-slice_fusion.2
  247.2 30.1 %collective-permute-done.3 = bf16[256,2048]{0,1:T(8,128)(2,1)} collective-permute-done((bf16[256,2048]{0,1:T(8,128)(2,1)}, bf16[256,2048]{0,1:T(8,128)(2,1)}, u32[]{:S(2)}, u32[]{:S(2)}) %collective-permute-start.3) | collective-permute-done | bytes 1048608 | tf_op jit(solution)/shard_map/ppermute | solution.py:15
  277.4 1.3 constant_dynamic-update-slice_fusion.1
  278.8 1.8 fusion.19
  280.6 8.7 %exponential_reduce_fusion = f32[8,2,256]{2,1,0:T(2,128)S(1)} fusion(bf16[1280,8,128,1]{0,2,3,1:T(8,128)(2,1)S(1)} %bitcast.63, pred[256,1280]{0,1:T(8,128)(4,1)S(1)} %fusion.8, bf16[256,8,2,64]{3,0,2,1:T(8,128)(2,1)} %bitcast.68, bf16[256,8,2,64]{3,0,2,1:T(8,128)(2,1)} %bitcast.66), kind=kOutput, calls=%fused_computation.4 | convolution fusion | flops 1365247232 | bytes 4014080 | tf_op jit(solution)/shard_map/sub | solution.py:86
  289.3 13.2 %fusion.4 = bf16[8,128,2,256]{3,1,2,0:T(8,128)(2,1)} fusion(bf16[1280,8,128,1]{0,2,3,1:T(8,128)(2,1)} %bitcast.65, f32[8,2,256]{2,1,0:T(2,128)S(1)} %exponential_reduce_fusion, bf16[1280,8,128,1]{0,2,3,1:T(8,128)(2,1)S(1)} %bitcast.64, pred[256,1280]{0,1:T(8,128)(4,1)S(1)} %fusion.8, bf16[256,8,2,64]{3,0,2,1:T(8,128)(2,1)} %bitcast.69, ...), kind=kOutput, calls=%fused_computation.14 | convolution fusion | flops 2713195776 | bytes 7684096 | tf_op jit(solution)/shard_map/kgtu,ukd->tkgd/dot_general | solution.py:89
  302.5 1.3 copy.35
  303.9 10.9 %multiply_reduce_fusion = (f32[256]{0:T(256)S(1)}, f32[256,5376]{1,0:T(8,128)S(1)}) fusion(bf16[256,2048]{0,1:T(8,128)(2,1)S(1)} %bitcast.62, bf16[2048,5376]{1,0:T(8,128)(2,1)} %all-gather.5.cloned.1.call-done), kind=kOutput, calls=%fused_computation.7 | convolution fusion | flops 5639897088 | bytes 28574720 | tf_op jit(solution)/shard_map/dot_general | solution.py:100
  314.9 2.1 fusion.3
  317.0 0.2 copy-done.1
  (25 shorter events, 0.4 us)
Async XLA Ops:
  6.5 1.8 copy-start
  6.5 59.1 %all-gather.3.cloned.1.call-start = ((), (), s32[]{:S(2)}) async-start(), calls=%async_computation | async-start | bytes 1548288 | tf_op jit(solution)/shard_map/all_gather | solution.py:98
  9.0 294.8 %all-gather.5.cloned.1.call-start = ((), (), s32[]{:S(2)}) async-start(), calls=%async_computation.1 | async-start | bytes 23396352 | tf_op jit(solution)/shard_map/all_gather | solution.py:99
  65.6 3.7 %copy-start.5 = (f32[128]{0:T(128)S(1)}, f32[128]{0:T(128)}, u32[]{:S(2)}) copy-start(f32[128]{0:T(128)} %param.11) | copy-start | bytes 1540
  69.5 14.1 %copy-start.2 = (bf16[1,256,2048]{2,1,0:T(8,128)(2,1)S(1)}, bf16[1,256,2048]{2,1,0:T(8,128)(2,1)}, u32[]{:S(2)}) copy-start(bf16[1,256,2048]{2,1,0:T(8,128)(2,1)} %param.7) | copy-start | bytes 3145732
  70.7 69.2 %collective-permute-start = (bf16[256,2048]{0,1:T(8,128)(2,1)}, bf16[256,2048]{0,1:T(8,128)(2,1)}, u32[]{:S(2)}, u32[]{:S(2)}) collective-permute-start(bf16[256,2048]{0,1:T(8,128)(2,1)} %pad_maximum_fusion), channel_id=1, source_target_pairs={{0,32},{8,40},{16,48},{24,56},{32,64},{40,72},{48,80},{56,88},{64,... | collective-permute-start | bytes 3145736 | tf_op jit(solution)/shard_map/ppermute | solution.py:15
  76.4 124.6 %collective-permute-start.1 = (bf16[256,2048]{0,1:T(8,128)(2,1)}, bf16[256,2048]{0,1:T(8,128)(2,1)}, u32[]{:S(2)}, u32[]{:S(2)}) collective-permute-start(bf16[256,2048]{0,1:T(8,128)(2,1)} %pad_maximum_fusion), channel_id=1, source_target_pairs={{0,24},{8,32},{16,40},{24,48},{32,56},{40,64},{48,72},{56,80},{64,... | collective-permute-start | bytes 3145736 | tf_op jit(solution)/shard_map/ppermute | solution.py:15
  78.3 167.6 %collective-permute-start.2 = (bf16[256,2048]{0,1:T(8,128)(2,1)}, bf16[256,2048]{0,1:T(8,128)(2,1)}, u32[]{:S(2)}, u32[]{:S(2)}) collective-permute-start(bf16[256,2048]{0,1:T(8,128)(2,1)} %pad_maximum_fusion), channel_id=1, source_target_pairs={{0,16},{8,24},{16,32},{24,40},{32,48},{40,56},{48,64},{56,72},{64,... | collective-permute-start | bytes 3145736 | tf_op jit(solution)/shard_map/ppermute | solution.py:15
  80.9 196.5 %collective-permute-start.3 = (bf16[256,2048]{0,1:T(8,128)(2,1)}, bf16[256,2048]{0,1:T(8,128)(2,1)}, u32[]{:S(2)}, u32[]{:S(2)}) collective-permute-start(bf16[256,2048]{0,1:T(8,128)(2,1)} %pad_maximum_fusion), channel_id=1, source_target_pairs={{0,8},{8,16},{16,24},{24,32},{32,40},{40,48},{48,56},{56,64},{64,7... | collective-permute-start | bytes 3145736 | tf_op jit(solution)/shard_map/ppermute | solution.py:15
  88.6 2.5 copy-start.3
  303.9 11.0 %copy-start.4 = (f32[5376]{0:T(1024)S(1)}, f32[5376]{0:T(1024)}, u32[]{:S(2)}) copy-start(f32[5376]{0:T(1024)} %param.13) | copy-start | bytes 64516
  314.8 2.3 copy-start.1
Sparse Core Ops, SparseCore 0:
  9.9 55.6 all-gather.2
  67.4 225.4 all-gather.4
where the time goes:
time: 325 us; the launch traced here: 324 us
  waiting for transfers between devices  238 us (73%)
  matrix products  32.8 us (10%)
  local copies, waits for them, and re-layouts  16.8 us (5%)
  between operations  13.7 us (4%)
  starting transfers between devices  12.7 us (4%)
  other arithmetic  9.65 us (3%)
    ppermute x4, waiting for transfers between devices, from_behind(): return lax.ppermute(block, axis, route)  182 us
    all_gather x1, waiting for transfers between devices, on_device(): partial_rows = lax.all_gather(mine, 'fsdp', axis=0, tiled=True)  56.5 us
    dot_general x1, matrix products, on_device(): jnp.einsum('kgtu,ukd->tkgd', probs, value_rows, preferred_element_type=jn...  13.2 us
    ppermute x4, starting transfers between devices, from_behind(): return lax.ppermute(block, axis, route)  12.6 us
    dot_general x1, matrix products, on_device(): projected = jnp.dot(arranged, all_rows, preferred_element_type=jnp.float32)  10.9 us
    unnamed x18, local copies, waits for them, and re-layouts  9.05 us
    sub x1, matrix products, on_device(): expd = jnp.exp(scores - top)  8.73 us
  transfers between devices with their start and end apart: 6, of which 5 were waited for; matrix products, arithmetic and copies ran while one was open for 13% of the time, Pallas kernels for 0%

commit v1 on v0

--- a/solution.py
+++ b/solution.py
@@ -95,7 +95,9 @@
     arranged = (
         outputs.reshape(tokens, n_fsdp, n_seq, each).transpose(0, 2, 1, 3).reshape(tokens, features)
     )
-    partial_rows = lax.all_gather(mine, "fsdp", axis=0, tiled=True)
+    partial_rows = jnp.concatenate(
+        lax.all_to_all(jnp.stack([mine] * lax.axis_size("fsdp")), "fsdp", 0, 0), axis=0
+    )
     all_rows = lax.all_gather(partial_rows, "seq", axis=0, tiled=True)
     projected = jnp.dot(arranged, all_rows, preferred_element_type=jnp.float32)
     meansq = jnp.mean(projected * projected, axis=-1, keepdims=True)

time: 325 us -> 293 us (0.902)
  waiting for transfers between devices: 238 us -> 178 us
  blocking collectives: 0 us -> 27.8 us
    all_gather x1 -> x0, waiting for transfers between devices: 56.5 us -> none  [on_device(): partial_rows = lax.all_gather(mine, 'fsdp', axis=0, tiled=True)]
    all_to_all x0 -> x1, blocking collectives: none -> 27.8 us  [on_device(): lax.all_to_all(jnp.stack([mine] * lax.axis_size('fsdp')), 'fsdp', 0, 0)]
    ppermute x4, waiting for transfers between devices: 182 us -> 178 us  [from_behind(): return lax.ppermute(block, axis, route)]
    unnamed x18 -> x20, local copies, waits for them, and re-layouts: 9.05 us -> 8.1 us
  transfers between devices with their start and end apart: 6 -> 5, of which waited for: 5 -> 4; matrix products, arithmetic and copies ran while one was open for 13% -> 15% of each run, Pallas kernels for 0% -> 0%
where the time goes in v1:
time: 293 us; the launch traced here: 292 us
  waiting for transfers between devices  178 us (61%)
  matrix products  32.8 us (11%)
  blocking collectives  27.8 us (9%)
  local copies, waits for them, and re-layouts  15.9 us (5%)
  starting transfers between devices  14.4 us (5%)
  between operations  13.7 us (5%)
  other arithmetic  9.56 us (3%)
    ppermute x4, waiting for transfers between devices, from_behind(): return lax.ppermute(block, axis, route)  178 us
    all_to_all x1, blocking collectives, on_device(): lax.all_to_all(jnp.stack([mine] * lax.axis_size('fsdp')), 'fsdp', 0, 0)  27.8 us
    ppermute x4, starting transfers between devices, from_behind(): return lax.ppermute(block, axis, route)  14.4 us
    dot_general x1, matrix products, on_device(): jnp.einsum('kgtu,ukd->tkgd', probs, value_rows, preferred_element_type=jn...  13.2 us
    dot_general x1, matrix products, on_device(): projected = jnp.dot(arranged, all_rows, preferred_element_type=jnp.float32)  10.9 us
    sub x1, matrix products, on_device(): expd = jnp.exp(scores - top)  8.73 us
    unnamed x20, local copies, waits for them, and re-layouts  8.1 us
  transfers between devices with their start and end apart: 5, of which 4 were waited for; matrix products, arithmetic and copies ran while one was open for 15% of the time, Pallas kernels for 0%

profile of v1, /device:TPU:64, one launch (start us, length us, event | category | flops | bytes accessed | tf_op | source)
XLA Modules:
  0.0 292.1 jit_solution(6995103683573693512)
XLA Ops:
  6.5 1.8 copy-done
  8.4 0.1 stack.2
  8.5 27.8 %all_to_all.5 = bf16[8,16,5376]{2,1,0:T(8,128)(2,1)} all-to-all(bf16[8,16,5376]{2,1,0:T(8,128)(2,1)S(1)} %stack.2), channel_id=1, replica_groups=mesh['dp'=2,'seq'=16,'fsdp'=8] {'fsdp'}, dimensions={0} | all-to-all | bytes 2752512 | tf_op jit(solution)/shard_map/all_to_all | solution.py:99
  36.3 0.1 compare_reduce_fusion
  36.4 0.1 add_select_fusion
  36.5 0.3 reduce-window.9
  36.8 0.1 slice.53
  36.9 0.5 copy.26
  37.5 0.1 slice_reduce_fusion
  37.7 0.1 fusion.11
  37.8 0.1 fusion.9
  37.9 0.3 multiply_cosine_fusion
  38.3 0.2 fusion.10
  38.4 0.1 subtract_convert_fusion.1
  38.6 1.0 pad_maximum_fusion
  39.7 6.4 %collective-permute-start = (bf16[256,2048]{0,1:T(8,128)(2,1)}, bf16[256,2048]{0,1:T(8,128)(2,1)}, u32[]{:S(2)}, u32[]{:S(2)}) collective-permute-start(bf16[256,2048]{0,1:T(8,128)(2,1)} %pad_maximum_fusion), channel_id=1, source_target_pairs={{0,32},{8,40},{16,48},{24,56},{32,64},{40,72},{48,80},{56,88},{64,... | collective-permute-start | bytes 3145736 | tf_op jit(solution)/shard_map/ppermute | solution.py:15
  46.1 1.9 collective-permute-start.1
  48.0 2.9 %collective-permute-start.2 = (bf16[256,2048]{0,1:T(8,128)(2,1)}, bf16[256,2048]{0,1:T(8,128)(2,1)}, u32[]{:S(2)}, u32[]{:S(2)}) collective-permute-start(bf16[256,2048]{0,1:T(8,128)(2,1)} %pad_maximum_fusion), channel_id=1, source_target_pairs={{0,16},{8,24},{16,32},{24,40},{32,48},{40,56},{48,64},{56,72},{64,... | collective-permute-start | bytes 3145736 | tf_op jit(solution)/shard_map/ppermute | solution.py:15
  50.9 3.2 %collective-permute-start.3 = (bf16[256,2048]{0,1:T(8,128)(2,1)}, bf16[256,2048]{0,1:T(8,128)(2,1)}, u32[]{:S(2)}, u32[]{:S(2)}) collective-permute-start(bf16[256,2048]{0,1:T(8,128)(2,1)} %pad_maximum_fusion), channel_id=1, source_target_pairs={{0,8},{8,16},{16,24},{24,32},{32,40},{40,48},{48,56},{56,64},{64,7... | collective-permute-start | bytes 3145736 | tf_op jit(solution)/shard_map/ppermute | solution.py:15
  54.1 0.1 copy.29
  54.2 0.1 copy.30
  54.3 0.2 convert_bitcast_fusion
  54.6 0.4 copy.41
  55.0 0.6 multiply_reduce_fusion.1
  55.6 0.7 copy.27
  56.3 1.3 add_rsqrt_fusion
  57.6 0.8 copy.28
  58.4 1.4 multiply_multiply_fusion
  59.9 0.8 subtract_convert_fusion
  60.6 1.3 copy.31
  61.9 1.2 copy.32
  63.2 0.1 pad_dynamic-slice_fusion
  63.2 0.5 fusion.8
  63.7 46.0 %collective-permute-done = bf16[256,2048]{0,1:T(8,128)(2,1)} collective-permute-done((bf16[256,2048]{0,1:T(8,128)(2,1)}, bf16[256,2048]{0,1:T(8,128)(2,1)}, u32[]{:S(2)}, u32[]{:S(2)}) %collective-permute-start) | collective-permute-done | bytes 1048608 | tf_op jit(solution)/shard_map/ppermute | solution.py:15
  109.7 1.3 constant_dynamic-update-slice_fusion.4
  111.0 59.3 %collective-permute-done.1 = bf16[256,2048]{0,1:T(8,128)(2,1)} collective-permute-done((bf16[256,2048]{0,1:T(8,128)(2,1)}, bf16[256,2048]{0,1:T(8,128)(2,1)}, u32[]{:S(2)}, u32[]{:S(2)}) %collective-permute-start.1) | collective-permute-done | bytes 1048608 | tf_op jit(solution)/shard_map/ppermute | solution.py:15
  170.3 1.3 constant_dynamic-update-slice_fusion.3
  171.6 43.6 %collective-permute-done.2 = bf16[256,2048]{0,1:T(8,128)(2,1)} collective-permute-done((bf16[256,2048]{0,1:T(8,128)(2,1)}, bf16[256,2048]{0,1:T(8,128)(2,1)}, u32[]{:S(2)}, u32[]{:S(2)}) %collective-permute-start.2) | collective-permute-done | bytes 1048608 | tf_op jit(solution)/shard_map/ppermute | solution.py:15
  215.2 1.3 constant_dynamic-update-slice_fusion.2
  216.5 29.0 %collective-permute-done.3 = bf16[256,2048]{0,1:T(8,128)(2,1)} collective-permute-done((bf16[256,2048]{0,1:T(8,128)(2,1)}, bf16[256,2048]{0,1:T(8,128)(2,1)}, u32[]{:S(2)}, u32[]{:S(2)}) %collective-permute-start.3) | collective-permute-done | bytes 1048608 | tf_op jit(solution)/shard_map/ppermute | solution.py:15
  245.5 1.3 constant_dynamic-update-slice_fusion.1
  246.9 1.8 fusion.19
  248.7 8.7 %exponential_reduce_fusion = f32[8,2,256]{2,1,0:T(2,128)S(1)} fusion(bf16[1280,8,128,1]{0,2,3,1:T(8,128)(2,1)S(1)} %bitcast.65, pred[256,1280]{0,1:T(8,128)(4,1)S(1)} %fusion.8, bf16[256,8,2,64]{3,0,2,1:T(8,128)(2,1)} %bitcast.70, bf16[256,8,2,64]{3,0,2,1:T(8,128)(2,1)} %bitcast.68), kind=kOutput, calls=%fused_computation.4 | convolution fusion | flops 1365247232 | bytes 4014080 | tf_op jit(solution)/shard_map/sub | solution.py:86
  257.5 13.2 %fusion.4 = bf16[8,128,2,256]{3,1,2,0:T(8,128)(2,1)} fusion(bf16[1280,8,128,1]{0,2,3,1:T(8,128)(2,1)} %bitcast.67, f32[8,2,256]{2,1,0:T(2,128)S(1)} %exponential_reduce_fusion, bf16[1280,8,128,1]{0,2,3,1:T(8,128)(2,1)S(1)} %bitcast.66, pred[256,1280]{0,1:T(8,128)(4,1)S(1)} %fusion.8, bf16[256,8,2,64]{3,0,2,1:T(8,128)(2,1)} %bitcast.71, ...), kind=kOutput, calls=%fused_computation.14 | convolution fusion | flops 2713195776 | bytes 7684096 | tf_op jit(solution)/shard_map/kgtu,ukd->tkgd/dot_general | solution.py:89
  270.6 1.3 copy.35
  272.0 10.9 %multiply_reduce_fusion = (f32[256]{0:T(256)S(1)}, f32[256,5376]{1,0:T(8,128)S(1)}) fusion(bf16[256,2048]{0,1:T(8,128)(2,1)S(1)} %bitcast.64, bf16[2048,5376]{1,0:T(8,128)(2,1)} %all-gather.2.cloned.1.call-done), kind=kOutput, calls=%fused_computation.7 | convolution fusion | flops 5639897088 | bytes 28574720 | tf_op jit(solution)/shard_map/dot_general | solution.py:102
  283.0 2.1 fusion.3
  285.1 0.2 copy-done.1
  (26 shorter events, 0.4 us)
Async XLA Ops:
  6.5 1.8 copy-start
  6.5 265.4 %all-gather.2.cloned.1.call-start = ((), (), s32[]{:S(2)}) async-start(), calls=%async_computation.1 | async-start | bytes 23396352 | tf_op jit(solution)/shard_map/all_gather | solution.py:101
  8.3 27.9 %copy-start.4 = (s32[1,4096]{1,0:T(1,128)S(1)}, s32[1,4096]{1,0:T(1,128)}, u32[]{:S(2)}) copy-start(s32[1,4096]{1,0:T(1,128)} %param.9) | copy-start | bytes 49156
  8.3 28.6 %copy-start.3 = (bf16[1,256,2048]{2,1,0:T(8,128)(2,1)S(1)}, bf16[1,256,2048]{2,1,0:T(8,128)(2,1)}, u32[]{:S(2)}) copy-start(bf16[1,256,2048]{2,1,0:T(8,128)(2,1)} %param.8) | copy-start | bytes 3145732
  36.2 2.0 copy-start.6
  38.4 15.9 %copy-start.2 = (bf16[1,256,2048]{2,1,0:T(8,128)(2,1)S(1)}, bf16[1,256,2048]{2,1,0:T(8,128)(2,1)}, u32[]{:S(2)}) copy-start(bf16[1,256,2048]{2,1,0:T(8,128)(2,1)} %param.7) | copy-start | bytes 3145732
  39.7 70.0 %collective-permute-start = (bf16[256,2048]{0,1:T(8,128)(2,1)}, bf16[256,2048]{0,1:T(8,128)(2,1)}, u32[]{:S(2)}, u32[]{:S(2)}) collective-permute-start(bf16[256,2048]{0,1:T(8,128)(2,1)} %pad_maximum_fusion), channel_id=1, source_target_pairs={{0,32},{8,40},{16,48},{24,56},{32,64},{40,72},{48,80},{56,88},{64,... | collective-permute-start | bytes 3145736 | tf_op jit(solution)/shard_map/ppermute | solution.py:15
  46.1 124.2 %collective-permute-start.1 = (bf16[256,2048]{0,1:T(8,128)(2,1)}, bf16[256,2048]{0,1:T(8,128)(2,1)}, u32[]{:S(2)}, u32[]{:S(2)}) collective-permute-start(bf16[256,2048]{0,1:T(8,128)(2,1)} %pad_maximum_fusion), channel_id=1, source_target_pairs={{0,24},{8,32},{16,40},{24,48},{32,56},{40,64},{48,72},{56,80},{64,... | collective-permute-start | bytes 3145736 | tf_op jit(solution)/shard_map/ppermute | solution.py:15
  48.0 167.3 %collective-permute-start.2 = (bf16[256,2048]{0,1:T(8,128)(2,1)}, bf16[256,2048]{0,1:T(8,128)(2,1)}, u32[]{:S(2)}, u32[]{:S(2)}) collective-permute-start(bf16[256,2048]{0,1:T(8,128)(2,1)} %pad_maximum_fusion), channel_id=1, source_target_pairs={{0,16},{8,24},{16,32},{24,40},{32,48},{40,56},{48,64},{56,72},{64,... | collective-permute-start | bytes 3145736 | tf_op jit(solution)/shard_map/ppermute | solution.py:15
  50.9 194.6 %collective-permute-start.3 = (bf16[256,2048]{0,1:T(8,128)(2,1)}, bf16[256,2048]{0,1:T(8,128)(2,1)}, u32[]{:S(2)}, u32[]{:S(2)}) collective-permute-start(bf16[256,2048]{0,1:T(8,128)(2,1)} %pad_maximum_fusion), channel_id=1, source_target_pairs={{0,8},{8,16},{16,24},{24,32},{32,40},{40,48},{48,56},{56,64},{64,7... | collective-permute-start | bytes 3145736 | tf_op jit(solution)/shard_map/ppermute | solution.py:15
  272.0 11.0 %copy-start.5 = (f32[5376]{0:T(1024)S(1)}, f32[5376]{0:T(1024)}, u32[]{:S(2)}) copy-start(f32[5376]{0:T(1024)} %param.13) | copy-start | bytes 64516
  283.0 2.3 copy-start.1
Sparse Core Ops, SparseCore 0:
  36.4 224.5 all-gather.1
